TPU v7x, 512 devices: a whole 4x4x16 slice. The times are simulated.
512 devices in a mesh: dp: 2 (over core), fsdp: 32 (over y, z_lo), tensor: 8 (over z_hi, x).
Axes of the slice: x: 4, y: 4, z: 16 (z_hi: 2, z_lo: 8; z = z_hi * 8 + z_lo), core: 2. Of those that a mesh axis runs over, the one named last changes fastest.
Arguments:
- tokens: bfloat16 [16384, 4096], P(('dp', 'fsdp', 'tensor')), may hold values from -40 to 40
- norm_gain: float32 [4096], replicated, may hold values from 0.5 to 1.5
- tile_values: bfloat16 [512, 128, 128], P(('fsdp', 'tensor')), may hold values from -0.25 to 0.25
- tile_rows: int32 [8, 64], P('tensor'), may hold values from 0 to 31, as said below
- tile_cols: int32 [8, 64], P('tensor'), may hold values from 0 to 13
- tile_counts: int32 [8, 32], P('tensor'), may hold values from 0 to 2, as said below
- grad_out: bfloat16 [16384, 14336], P(('dp', 'fsdp'), 'tensor'), may hold values from -3 to 3
Outputs:
- mixed: bfloat16 [16384, 14336], P(('dp', 'fsdp'), 'tensor')
- grad_x: bfloat16 [16384, 4096], P(('dp', 'fsdp', 'tensor'))
- grad_gain: float32 [4096], replicated
- grad_tiles: float32 [512, 128, 128], P(('fsdp', 'tensor'))
Inputs may be any that keep to these rules, and one draw needn't show every extreme that they name: `tile_counts`: for each tensor index the counts over the 32 fsdp shards sum to 56, and some shard holds exactly 2. `tile_rows`: within one tensor index the (row, column) pairs of held slots are all different.
All inputs are finite; a program needn't handle non-finite values.
Results may differ from a plain program's by a relative error of at most 0.013.
Values may be sent and summed in bfloat16 or wider, within the bound.
A program may use at most 128 MiB of HBM per device.

v0:
```python
import jax
import jax.numpy as jnp
from jax import lax
from jax.sharding import PartitionSpec as P


def tile_forward(group_rows, values, rows_list, cols_list, col_tiles):
    tile_size = values.shape[1]
    blocks = group_rows.reshape(group_rows.shape[0], -1, tile_size)
    picked = jnp.take(blocks, rows_list, axis=1)
    product = jnp.einsum("tsk,skn->tsn", picked, values, preferred_element_type=jnp.float32)
    placed = (
        jnp.zeros((group_rows.shape[0], col_tiles, tile_size), jnp.float32)
        .at[:, cols_list]
        .add(product)
    )
    return placed.reshape(group_rows.shape[0], col_tiles * tile_size)


def tile_backward(grad_rows, values, rows_list, cols_list, row_tiles):
    tile_size = values.shape[1]
    blocks = grad_rows.reshape(grad_rows.shape[0], -1, tile_size)
    picked = jnp.take(blocks, cols_list, axis=1)
    product = jnp.einsum("tsn,skn->tsk", picked, values, preferred_element_type=jnp.float32)
    placed = (
        jnp.zeros((grad_rows.shape[0], row_tiles, tile_size), jnp.float32)
        .at[:, rows_list]
        .add(product)
    )
    return placed.reshape(grad_rows.shape[0], row_tiles * tile_size)


def per_device(tokens, norm_gain, tile_values, tile_rows, tile_cols, tile_counts, grad_out):
    tile_size = tile_values.shape[1]
    slot_cap = tile_values.shape[0]
    row_tiles = tokens.shape[1] // tile_size
    col_tiles = grad_out.shape[1] // tile_size
    rows_list = tile_rows[0]
    cols_list = tile_cols[0]
    shard_counts = tile_counts[0]
    held_all = (jnp.arange(slot_cap)[None, :] < shard_counts[:, None]).reshape(-1)
    own_held = jnp.arange(slot_cap) < shard_counts[lax.axis_index("fsdp")]
    local_float = tokens.astype(jnp.float32)
    inv_rms = lax.rsqrt(jnp.mean(local_float * local_float, axis=1, keepdims=True) + 1e-05)
    scaled = local_float * inv_rms
    normed = (scaled * norm_gain).astype(jnp.bfloat16)
    group_rows = lax.all_gather(normed, "tensor", axis=0, tiled=True)
    gathered = lax.all_gather(tile_values, "fsdp", axis=0, tiled=True)
    kept_values = jnp.where(held_all[:, None, None], gathered, jnp.zeros_like(gathered))
    outputs = tile_forward(group_rows, kept_values, rows_list, cols_list, col_tiles)
    mixed = outputs.astype(jnp.bfloat16)
    input_grad = lax.psum_scatter(
        tile_backward(grad_out, kept_values, rows_list, cols_list, row_tiles).astype(jnp.bfloat16),
        "tensor",
        scatter_dimension=0,
        tiled=True,
    ).astype(jnp.float32)
    x_blocks = group_rows.reshape(group_rows.shape[0], row_tiles, tile_size)
    g_blocks = grad_out.reshape(grad_out.shape[0], col_tiles, tile_size)
    picked_x = jnp.take(x_blocks, rows_list, axis=1)
    picked_g = jnp.take(g_blocks, cols_list, axis=1)
    grad_shard = lax.psum_scatter(
        jnp.einsum("tsk,tsn->skn", picked_x, picked_g, preferred_element_type=jnp.float32),
        "fsdp",
        scatter_dimension=0,
        tiled=True,
    )
    grad_shard = jnp.where(own_held[:, None, None], grad_shard, jnp.zeros_like(grad_shard))
    grad_tiles = lax.psum(grad_shard, "dp")
    gain_part = jnp.sum(input_grad * scaled, axis=0)
    grad_gain = lax.psum(gain_part, ("dp", "fsdp", "tensor"))
    hidden_grad = input_grad * norm_gain
    grad_x = (
        inv_rms * (hidden_grad - scaled * jnp.mean(hidden_grad * scaled, axis=1, keepdims=True))
    ).astype(jnp.bfloat16)
    return (mixed, grad_x, grad_gain, grad_tiles)


def solution(mesh):
    placed = (
        P(("dp", "fsdp", "tensor"), None),
        P(),
        P(("fsdp", "tensor"), None, None),
        P("tensor", None),
        P("tensor", None),
        P("tensor", None),
        P(("dp", "fsdp"), "tensor"),
    )
    return jax.shard_map(
        per_device,
        mesh=mesh,
        in_specs=placed,
        out_specs=(
            P(("dp", "fsdp"), "tensor"),
            P(("dp", "fsdp", "tensor"), None),
            P(),
            P(("fsdp", "tensor"), None, None),
        ),
        check_vma=False,
    )
```

profile of v0, /device:TPU:1, one launch (start us, length us, event | category | flops | bytes accessed | tf_op | source)
XLA Modules:
  0.0 848.5 jit_solution(9026113694259479338)
XLA Ops:
  7.2 0.7 all-gather.3.cloned.1.call-update
  7.9 1.5 copy.32
  9.4 0.6 copy.33
  10.0 0.7 iota_compare_fusion
  10.9 0.7 compare_select_fusion
  11.6 3.1 gather_fusion.1
  14.7 207.7 %all-gather.3.cloned.1.call-done = bf16[64,128,128]{2,1,0:T(8,128)(2,1)} async-done(((bf16[2,128,128]{2,1,0:T(8,128)(2,1)}), bf16[64,128,128]{2,1,0:T(8,128)(2,1)}) %all-gather.3.cloned.1.call-update) | async-done | bytes 2097168 | tf_op jit(solution)/shard_map/all_gather | solution.py:48
  222.3 7.4 fusion.2
  229.8 2.4 broadcast_in_dim.57
  232.2 19.4 %scatter_fusion.1 = f32[256,32,128]{2,0,1:T(8,128)} fusion(f32[256,32,128]{2,0,1:T(8,128)} %broadcast_in_dim.57, s32[64]{0:T(128)S(1)} %fusion.18, f32[64,256,128]{2,1,0:T(8,128)} %fusion.2), kind=kCustom, calls=%fused_computation.3 | custom fusion | flops 2097152 | bytes 25166080 | tf_op jit(solution)/shard_map/scatter-add | solution.py:28
  251.6 2.5 convert_element_type.28
  254.1 2.9 copy.34
  257.0 4.1 copy.39
  261.4 162.8 %reduce-scatter.7.cloned.1.call-done = bf16[32,4096]{1,0:T(8,128)(2,1)} async-done(((bf16[256,4096]{1,0:T(8,128)(2,1)}), bf16[32,4096]{1,0:T(8,128)(2,1)}) %reduce-scatter.7.cloned.1.call-update) | async-done | bytes 262160 | tf_op jit(solution)/shard_map/reduce_scatter | solution.py:52
  424.3 1.3 fusion.16
  425.5 1.9 fusion.12
  427.6 109.9 %all-gather.5.cloned.1.call-done = bf16[256,4096]{1,0:T(8,128)(2,1)} async-done(((bf16[32,4096]{1,0:T(8,128)(2,1)}), bf16[256,4096]{1,0:T(8,128)(2,1)}) %all-gather.5.cloned.1.call-update) | async-done | bytes 2097168 | tf_op jit(solution)/shard_map/all_gather | solution.py:47
  537.5 4.1 copy.29
  541.6 3.2 copy.30
  544.8 3.0 gather_fusion
  547.8 7.0 fusion
  554.9 0.6 copy-done.3
  555.5 0.6 constant_dynamic-slice_fusion
  556.1 0.6 iota_compare_fusion.1
  556.7 103.2 %psum.14 = f32[4096]{0:T(1024)} all-reduce(f32[4096]{0:T(1024)S(1)} %get-tuple-element.18), channel_id=1, replica_groups=mesh['dp'=2,'fsdp'=32,'tensor'=8] {'dp','fsdp','tensor'}, use_global_device_ids=true, to_apply=%region_6.9 | all-reduce | flops 4096 | bytes 32768 | tf_op jit(solution)/shard_map/psum | solution.py:71
  659.9 119.5 %reduce-scatter.5.cloned.1.call-done = f32[2,128,128]{2,1,0:T(8,128)} async-done(((f32[64,128,128]{2,1,0:T(8,128)}), f32[2,128,128]{2,1,0:T(8,128)}) %reduce-scatter.5.cloned.1.call-update) | async-done | bytes 131088 | tf_op jit(solution)/shard_map/reduce_scatter | solution.py:62
  779.5 1.6 broadcast_select_fusion.9
  781.1 6.7 fusion.5
  788.0 12.4 %scatter_fusion = f32[256,14,128]{2,0,1:T(8,128)S(1)} fusion(f32[256,14,128]{2,0,1:T(8,128)S(1)} %broadcast_in_dim.54, s32[64]{0:T(128)S(1)} %fusion.17, f32[64,256,128]{2,1,0:T(8,128)} %fusion.5), kind=kCustom, calls=%fused_computation.2 | custom fusion | flops 2097152 | bytes 25166080 | tf_op jit(solution)/shard_map/scatter-add | solution.py:15
  801.2 1.4 copy.37
  802.5 37.8 %all-reduce.2.cloned.1.call-done = f32[2,128,128]{2,1,0:T(8,128)} async-done(((f32[2,128,128]{2,1,0:T(8,128)}), f32[2,128,128]{2,1,0:T(8,128)}) %all-reduce.2.cloned.1.call-update) | async-done | bytes 131088 | tf_op jit(solution)/shard_map/psum | solution.py:69
  840.4 1.6 copy.44
  (33 shorter events, 1.5 us)
Async XLA Ops:
  7.2 215.2 %all-gather.3.cloned.1.call-start = ((), (), s32[]{:S(2)}) async-start(), calls=%async_computation.2 | async-start | bytes 2162688 | tf_op jit(solution)/shard_map/all_gather | solution.py:48
  7.9 416.4 %reduce-scatter.7.cloned.1.call-start = ((), (), s32[]{:S(2)}) async-start(), calls=%async_computation.6 | async-start | bytes 2359296 | tf_op jit(solution)/shard_map/reduce_scatter | solution.py:52
  11.6 3.1 copy-start.4
  11.6 3.1 copy-start.5
  257.0 4.2 copy-start.1
  257.0 167.2 %copy-start.2 = (f32[4096]{0:T(1024)S(1)}, f32[4096]{0:T(1024)}, u32[]{:S(2)}) copy-start(f32[4096]{0:T(1024)} %param.12) | copy-start | bytes 49156
  261.2 276.3 %all-gather.5.cloned.1.call-start = ((), (), s32[]{:S(2)}) async-start(), calls=%async_computation.3 | async-start | bytes 2359296 | tf_op jit(solution)/shard_map/all_gather | solution.py:47
  427.5 352.0 %reduce-scatter.5.cloned.1.call-start = ((), (), s32[]{:S(2)}) async-start(), calls=%async_computation.4 | async-start | bytes 4325376 | tf_op jit(solution)/shard_map/reduce_scatter | solution.py:62
  554.8 0.7 copy-start.3
  554.8 226.3 %copy-start = (bf16[64,128,128]{2,1,0:T(8,128)(2,1)S(1)}, bf16[64,128,128]{2,1,0:T(8,128)(2,1)}, u32[]{:S(2)}) copy-start(bf16[64,128,128]{2,1,0:T(8,128)(2,1)} %all-gather.3.cloned.1.call-done) | copy-start | bytes 6291460
  554.9 285.5 %all-reduce.2.cloned.1.call-start = ((), (), s32[]{:S(2)}) async-start(), calls=%async_computation.5 | async-start | bytes 262144 | tf_op jit(solution)/shard_map/psum | solution.py:69
Sparse Core Ops, SparseCore 0:
  10.1 212.2 all-gather.2
  261.3 162.8 reduce-scatter.6
  428.5 108.9 all-gather.4
  555.0 224.4 reduce-scatter.4
  783.0 57.3 all-reduce.1
where the time goes:
time: 849 us; the launch traced here: 848 us
  waiting for transfers between devices  639 us (75%)
  blocking collectives  103 us (12%)
  other arithmetic  41.6 us (5%)
  local copies, waits for them, and re-layouts  29.9 us (4%)
  matrix products  21.2 us (2%)
  between operations  13.9 us (2%)
    all_gather x1, waiting for transfers between devices, per_device(): gathered = lax.all_gather(tile_values, 'fsdp', axis=0, tiled=True)  208 us
    reduce_scatter x1, waiting for transfers between devices, per_device(): lax.psum_scatter(tile_backward(grad_out, kept_values, rows_list, cols_lis...  163 us
    reduce_scatter x1, waiting for transfers between devices, per_device(): lax.psum_scatter(jnp.einsum('tsk,tsn->skn', picked_x, picked_g, preferred...  120 us
    all_gather x1, waiting for transfers between devices, per_device(): group_rows = lax.all_gather(normed, 'tensor', axis=0, tiled=True)  110 us
    psum x1, blocking collectives, per_device(): grad_gain = lax.psum(gain_part, ('dp', 'fsdp', 'tensor'))  103 us
    psum x1, waiting for transfers between devices, per_device(): grad_tiles = lax.psum(grad_shard, 'dp')  37.8 us
    scatter-add x1, other arithmetic, tile_backward(): placed = jnp.zeros((grad_rows.shape[0], row_tiles, tile_size), jnp.float3...  19.4 us
  transfers between devices with their start and end apart: 5, of which 5 were waited for; matrix products, arithmetic and copies ran while one was open for 3% of the time, Pallas kernels for 0%

commit v1 on v0

--- a/solution.py
+++ b/solution.py
@@ -68,7 +68,7 @@
     grad_shard = jnp.where(own_held[:, None, None], grad_shard, jnp.zeros_like(grad_shard))
     grad_tiles = lax.psum(grad_shard, "dp")
     gain_part = jnp.sum(input_grad * scaled, axis=0)
-    grad_gain = lax.psum(gain_part, ("dp", "fsdp", "tensor"))
+    grad_gain = lax.psum(lax.psum(gain_part, ("fsdp", "tensor")), "dp")
     hidden_grad = input_grad * norm_gain
     grad_x = (
         inv_rms * (hidden_grad - scaled * jnp.mean(hidden_grad * scaled, axis=1, keepdims=True))

time: 849 us -> 2670 us (3.14)
  blocking collectives: 103 us -> 2050 us
  waiting for transfers between devices: 639 us -> 516 us
    psum x1 -> x2, blocking collectives: 103 us -> 2050 us  [per_device(): grad_gain = lax.psum(lax.psum(gain_part, ('fsdp', 'tensor')), 'dp')]
    reduce_scatter x1, waiting for transfers between devices: 120 us -> 0.01 us  [per_device(): lax.psum_scatter(jnp.einsum('tsk,tsn->skn', picked_x, picked_g, preferred...]
  transfers between devices with their start and end apart: 5 -> 5, of which waited for: 5 -> 4; matrix products, arithmetic and copies ran while one was open for 3% -> 1% of each run, Pallas kernels for 0% -> 0%
where the time goes in v1:
time: 2670 us
  blocking collectives  2050 us (77%)
  waiting for transfers between devices  516 us (19%)
  other arithmetic  41.6 us (2%)
  local copies, waits for them, and re-layouts  29.9 us (1%)
    psum x2, blocking collectives, per_device(): grad_gain = lax.psum(lax.psum(gain_part, ('fsdp', 'tensor')), 'dp')  2050 us
    all_gather x1, waiting for transfers between devices, per_device(): gathered = lax.all_gather(tile_values, 'fsdp', axis=0, tiled=True)  208 us
    reduce_scatter x1, waiting for transfers between devices, per_device(): lax.psum_scatter(tile_backward(grad_out, kept_values, rows_list, cols_lis...  163 us
    all_gather x1, waiting for transfers between devices, per_device(): group_rows = lax.all_gather(normed, 'tensor', axis=0, tiled=True)  110 us
  transfers between devices with their start and end apart: 5, of which 4 were waited for; matrix products, arithmetic and copies ran while one was open for 1% of the time, Pallas kernels for 0%

profile of v1, /device:TPU:1, one launch (start us, length us, event | category | flops | bytes accessed | tf_op | source)
XLA Modules:
  0.0 2668.5 jit_solution(7253578083926251606)
XLA Ops:
  7.2 0.7 all-gather.3.cloned.1.call-update
  7.9 1.5 copy.32
  9.4 0.6 copy.33
  10.0 0.7 iota_compare_fusion
  10.9 0.7 compare_select_fusion
  11.6 3.1 gather_fusion.1
  14.7 207.7 %all-gather.3.cloned.1.call-done = bf16[64,128,128]{2,1,0:T(8,128)(2,1)} async-done(((bf16[2,128,128]{2,1,0:T(8,128)(2,1)}), bf16[64,128,128]{2,1,0:T(8,128)(2,1)}) %all-gather.3.cloned.1.call-update) | async-done | bytes 2097168 | tf_op jit(solution)/shard_map/all_gather | solution.py:48
  222.3 7.4 fusion.2
  229.8 2.4 broadcast_in_dim.57
  232.2 19.4 scatter_fusion.1
  251.6 2.5 convert_element_type.28
  254.1 2.9 copy.34
  257.0 4.1 copy.39
  261.4 163.2 %reduce-scatter.7.cloned.1.call-done = bf16[32,4096]{1,0:T(8,128)(2,1)} async-done(((bf16[256,4096]{1,0:T(8,128)(2,1)}), bf16[32,4096]{1,0:T(8,128)(2,1)}) %reduce-scatter.7.cloned.1.call-update) | async-done | bytes 262160 | tf_op jit(solution)/shard_map/reduce_scatter | solution.py:52
  424.6 1.3 fusion.16
  425.9 1.9 fusion.12
  428.0 109.9 %all-gather.5.cloned.1.call-done = bf16[256,4096]{1,0:T(8,128)(2,1)} async-done(((bf16[32,4096]{1,0:T(8,128)(2,1)}), bf16[256,4096]{1,0:T(8,128)(2,1)}) %all-gather.5.cloned.1.call-update) | async-done | bytes 2097168 | tf_op jit(solution)/shard_map/all_gather | solution.py:47
  537.8 4.1 copy.29
  541.9 3.2 copy.30
  545.1 3.0 gather_fusion
  548.2 7.0 fusion
  555.3 0.6 copy-done.3
  555.8 0.6 constant_dynamic-slice_fusion
  556.4 0.6 iota_compare_fusion.1
  557.1 1818.8 %psum.21 = f32[4096]{0:T(1024)S(1)} all-reduce(f32[4096]{0:T(1024)S(1)} %get-tuple-element.18), channel_id=1, replica_groups=mesh['dp'=2,'fsdp'=32,'tensor'=8] {'fsdp','tensor'}, use_global_device_ids=true, to_apply=%region_6.9 | all-reduce | flops 4096 | bytes 32768 | tf_op jit(solution)/shard_map/psum | solution.py:71
  2375.9 226.6 %psum.22 = f32[4096]{0:T(1024)} all-reduce(f32[4096]{0:T(1024)S(1)} %psum.21), channel_id=1, replica_groups=mesh['dp'=2,'fsdp'=32,'tensor'=8] {'dp'}, use_global_device_ids=true, to_apply=%region_7.10 | all-reduce | flops 4096 | bytes 32768 | tf_op jit(solution)/shard_map/psum | solution.py:71
  2602.6 1.6 broadcast_select_fusion.9
  2604.2 6.7 fusion.5
  2611.1 12.4 scatter_fusion
  2624.2 1.4 copy.37
  2625.6 34.8 %all-reduce.2.cloned.1.call-done = f32[2,128,128]{2,1,0:T(8,128)} async-done(((f32[2,128,128]{2,1,0:T(8,128)}), f32[2,128,128]{2,1,0:T(8,128)}) %all-reduce.2.cloned.1.call-update) | async-done | bytes 131088 | tf_op jit(solution)/shard_map/psum | solution.py:69
  2660.4 1.6 copy.44
  (34 shorter events, 1.5 us)
Async XLA Ops:
  7.2 215.2 %all-gather.3.cloned.1.call-start = ((), (), s32[]{:S(2)}) async-start(), calls=%async_computation.2 | async-start | bytes 2162688 | tf_op jit(solution)/shard_map/all_gather | solution.py:48
  7.9 416.7 %reduce-scatter.7.cloned.1.call-start = ((), (), s32[]{:S(2)}) async-start(), calls=%async_computation.6 | async-start | bytes 2359296 | tf_op jit(solution)/shard_map/reduce_scatter | solution.py:52
  11.6 3.1 copy-start.4
  11.6 3.1 copy-start.5
  257.0 4.2 copy-start.1
  257.0 167.6 %copy-start.2 = (f32[4096]{0:T(1024)S(1)}, f32[4096]{0:T(1024)}, u32[]{:S(2)}) copy-start(f32[4096]{0:T(1024)} %param.12) | copy-start | bytes 49156
  261.2 276.6 %all-gather.5.cloned.1.call-start = ((), (), s32[]{:S(2)}) async-start(), calls=%async_computation.3 | async-start | bytes 2359296 | tf_op jit(solution)/shard_map/all_gather | solution.py:47
  427.9 2174.7 %reduce-scatter.5.cloned.1.call-start = ((), (), s32[]{:S(2)}) async-start(), calls=%async_computation.4 | async-start | bytes 4325376 | tf_op jit(solution)/shard_map/reduce_scatter | solution.py:62
  555.2 0.7 copy-start.3
  555.2 2049.0 %copy-start = (bf16[64,128,128]{2,1,0:T(8,128)(2,1)S(1)}, bf16[64,128,128]{2,1,0:T(8,128)(2,1)}, u32[]{:S(2)}) copy-start(bf16[64,128,128]{2,1,0:T(8,128)(2,1)} %all-gather.3.cloned.1.call-done) | copy-start | bytes 6291460
  555.2 2105.2 %all-reduce.2.cloned.1.call-start = ((), (), s32[]{:S(2)}) async-start(), calls=%async_computation.5 | async-start | bytes 262144 | tf_op jit(solution)/shard_map/psum | solution.py:69
Sparse Core Ops, SparseCore 0:
  10.1 212.2 all-gather.2
  261.3 163.2 reduce-scatter.6
  428.9 108.8 all-gather.4
  555.3 224.9 reduce-scatter.4
  2604.3 56.0 all-reduce.1
